TPU v7x, 32 devices: a whole 2x2x4 slice. The times are simulated.
32 devices in a mesh: sec: 4 (over y, x), dev: 8 (over z, core).
Axes of the slice: x: 2, y: 2, z: 4, core: 2. Of those that a mesh axis runs over, the one named last changes fastest.
Arguments:
- hidden: bfloat16 [512, 3584], P(('sec', 'dev')), may hold values from -6 to 6
- expert_ids: int32 [512, 8], P(('sec', 'dev')), may hold values from 0 to 31, all different within a row; in each aligned block of 16 rows (0 to 15, 16 to 31, ...) at most 8 rows name the same one
- route_weights: float32 [512, 8], P(('sec', 'dev')), may hold values from 0.1 to 1
- w_gate_up: bfloat16 [32, 3584, 2048], P(('sec', 'dev')), may hold values from -0.09375 to 0.09375
- w_down: bfloat16 [32, 1024, 3584], P(('sec', 'dev')), may hold values from -0.1875 to 0.1875
- query_latent: bfloat16 [128, 128, 512], P(('sec', 'dev')), may hold values from -400 to 400
- query_rope: bfloat16 [128, 64, 128], P(('sec', 'dev')), may hold values from -6 to 6
- latent_cache: bfloat16 [128, 512, 512], P(('sec', 'dev')), may hold values from -4 to 4
- rope_cache: bfloat16 [128, 64, 512], P(('sec', 'dev')), may hold values from -6 to 6
- cache_lengths: int32 [128], P(('sec', 'dev')), may hold values from 64 to 512
Outputs:
- moe_out: bfloat16 [512, 3584], P(('sec', 'dev'))
- expert_load: float32 [32], replicated
- attention_out: bfloat16 [128, 128, 512], P(('sec', 'dev'))
Inputs may be any that keep to these rules, and one draw needn't show every extreme that they name: `expert_ids`: in the rows of one device no expert is named more than 8 times; in some device's rows some expert is named exactly 8 times.
All inputs are finite; a program needn't handle non-finite values.
Results may differ from a plain program's by a relative error of at most 0.008.
Values may be sent and summed in bfloat16 or wider, within the bound.
A program may use at most 128 MiB of HBM per device.

v0:
```python
import jax
import jax.numpy as jnp
from jax import lax
from jax.sharding import PartitionSpec as P


def attend(query_latent, query_rope, latent_cache, rope_cache, cache_lengths):
    factor = (query_latent.shape[2] + query_rope.shape[1]) ** (-0.5)
    scores = jnp.einsum(
        "rhc,rtc->rht", query_latent, latent_cache, preferred_element_type=jnp.float32
    )
    scores = scores + jnp.einsum(
        "rph,rpt->rht", query_rope, rope_cache, preferred_element_type=jnp.float32
    )
    scores = scores * factor
    positions = jnp.arange(latent_cache.shape[1], dtype=jnp.int32)
    live_mask = positions[None, None, :] < cache_lengths[:, None, None]
    scores = jnp.where(live_mask, scores, -1e30)
    highest = jnp.max(scores, axis=-1, keepdims=True)
    powers = jnp.exp(scores - highest)
    attention_weights = (powers / jnp.sum(powers, axis=-1, keepdims=True)).astype(jnp.bfloat16)
    result = jnp.einsum(
        "rht,rtc->rhc", attention_weights, latent_cache, preferred_element_type=jnp.float32
    )
    return result.astype(jnp.bfloat16)


def expert_apply(received, w_gate_up, w_down):
    shape_in = received.shape
    flat_rows = received.reshape(-1, shape_in[-1])
    projected = jnp.dot(flat_rows, w_gate_up[0], preferred_element_type=jnp.float32)
    hidden_units = w_down.shape[1]
    activated = (jax.nn.silu(projected[:, :hidden_units]) * projected[:, hidden_units:]).astype(
        jnp.bfloat16
    )
    produced = jnp.dot(activated, w_down[0], preferred_element_type=jnp.float32).astype(
        jnp.bfloat16
    )
    return produced.reshape(shape_in)


def per_device(
    hidden,
    expert_ids,
    route_weights,
    w_gate_up,
    w_down,
    query_latent,
    query_rope,
    latent_cache,
    rope_cache,
    cache_lengths,
):
    row_count, model_width = hidden.shape
    top_count = expert_ids.shape[1]
    sections = lax.axis_size("sec")
    members = lax.axis_size("dev")
    experts = sections * members
    capacity = 2 * row_count * top_count // experts
    flat_ids = expert_ids.reshape(-1)
    expert_range = jnp.arange(experts, dtype=jnp.int32)
    onehot = (flat_ids[:, None] == expert_range[None, :]).astype(jnp.int32)
    earlier = jnp.cumsum(onehot, axis=0) - onehot
    rank_in = jnp.sum(earlier * onehot, axis=1)
    slot_index = flat_ids * capacity + rank_in
    slot_range = jnp.arange(experts * capacity, dtype=jnp.int32)
    placer = (slot_range[:, None] == slot_index[None, :]).reshape(
        experts * capacity, row_count, top_count
    )
    placer = jnp.sum(placer.astype(jnp.int32), axis=2).astype(jnp.bfloat16)
    outgoing = jnp.dot(placer, hidden, preferred_element_type=jnp.float32).astype(jnp.bfloat16)
    outgoing = outgoing.reshape(experts, capacity, model_width)
    counts = jnp.sum(onehot, axis=0).astype(jnp.float32)
    totals = lax.psum(counts, ("sec", "dev"))
    expert_load = totals / float(row_count * top_count)
    returned = lax.all_to_all(
        expert_apply(
            lax.all_to_all(outgoing, ("sec", "dev"), split_axis=0, concat_axis=0, tiled=True),
            w_gate_up,
            w_down,
        ),
        ("sec", "dev"),
        split_axis=0,
        concat_axis=0,
        tiled=True,
    )
    picked = returned.reshape(experts * capacity, model_width)[slot_index]
    picked = picked.reshape(row_count, top_count, model_width)
    moe_out = jnp.einsum("rk,rkd->rd", route_weights, picked.astype(jnp.float32)).astype(
        jnp.bfloat16
    )
    attention_out = attend(query_latent, query_rope, latent_cache, rope_cache, cache_lengths)
    return (moe_out, expert_load, attention_out)


def solution(mesh):
    return jax.shard_map(
        per_device,
        mesh=mesh,
        in_specs=(
            P(("sec", "dev"), None),
            P(("sec", "dev"), None),
            P(("sec", "dev"), None),
            P(("sec", "dev"), None, None),
            P(("sec", "dev"), None, None),
            P(("sec", "dev"), None, None),
            P(("sec", "dev"), None, None),
            P(("sec", "dev"), None, None),
            P(("sec", "dev"), None, None),
            P(("sec", "dev")),
        ),
        out_specs=(P(("sec", "dev"), None), P(), P(("sec", "dev"), None, None)),
        check_vma=False,
    )
```

profile of v0, /device:TPU:0, one launch (start us, length us, event | category | flops | bytes accessed | tf_op | source)
XLA Modules:
  0.0 142.1 jit_solution(13405597893169225870)
XLA Ops:
  0.6 0.0 copy-start
  0.6 0.9 copy.17
  1.6 0.1 eq.30
  1.6 0.1 fusion.23
  1.7 0.2 reduce_window_sum.11
  1.9 0.2 fusion.24
  2.1 0.1 reduce_sum.41
  2.2 0.1 convert_reduce_fusion
  2.3 1.6 %fusion.8 = bf16[32,8,3584]{2,1,0:T(8,128)(2,1)S(1)} fusion(bf16[16,3584]{1,0:T(8,128)(2,1)} %param.10, s32[256,16]{0,1:T(8,128)S(1)} %convert_reduce_fusion), kind=kOutput, calls=%fused_computation.8 | convolution fusion | flops 30281728 | bytes 1966080 | tf_op jit(solution)/shard_map/dot_general | solution.py:71
  3.9 0.0 slice-start
  3.9 51.5 %all_to_all.10 = bf16[32,8,3584]{2,1,0:T(8,128)(2,1)S(1)} all-to-all(bf16[32,8,3584]{2,1,0:T(8,128)(2,1)S(1)} %fusion.8), channel_id=1, replica_groups=mesh['sec'=4,'dev'=8] {'sec','dev'}, dimensions={0} | all-to-all | bytes 3670016 | tf_op jit(solution)/shard_map/all_to_all | solution.py:78
  55.4 7.4 %fusion.1 = f32[256,2048]{1,0:T(8,128)S(1)} fusion(bf16[1,3584,2048]{2,1,0:T(8,128)(2,1)} %param.13, bf16[32,8,3584]{2,1,0:T(8,128)(2,1)S(1)} %all_to_all.10), kind=kOutput, calls=%fused_computation.2 | convolution fusion | flops 3758096384 | bytes 18612224 | tf_op jit(solution)/shard_map/dot_general | solution.py:31
  62.8 0.0 slice-done
  62.9 0.0 slice-done.1
  62.9 3.3 %fusion.9 = bf16[32,8,3584]{2,1,0:T(8,128)(2,1)} fusion(bf16[1,1024,3584]{2,1,0:T(8,128)(2,1)S(1)} %bitcast.43, f32[256,2048]{1,0:T(8,128)S(1)} %fusion.1), kind=kOutput, calls=%fused_computation.9 | convolution fusion | flops 1881538560 | bytes 11272192 | tf_op jit(solution)/shard_map/dot_general | solution.py:36
  66.2 3.6 %all-to-all-start.1 = ((bf16[32,8,3584]{2,1,0:T(8,128)(2,1)}), bf16[32,8,3584]{2,1,0:T(8,128)(2,1)}, u32[]{:S(2)}, u32[]{:S(2)}) async-start(bf16[32,8,3584]{2,1,0:T(8,128)(2,1)} %fusion.9), calls=%async_computation.1 | async-start | bytes 3670016 | tf_op jit(solution)/shard_map/all_to_all | solution.py:76
  69.8 0.0 copy-start.2
  69.8 0.0 copy-start.3
  69.8 63.3 %psum.7 = f32[32]{0:T(128)S(1)} all-reduce(f32[32]{0:T(128)S(1)} %convert_element_type.38), channel_id=1, replica_groups=mesh['sec'=4,'dev'=8] {'sec','dev'}, use_global_device_ids=true, to_apply=%region_4.5 | all-reduce | flops 32 | bytes 256 | tf_op jit(solution)/shard_map/psum | solution.py:74
  133.1 0.1 mul.41
  133.2 0.0 copy-done.4
  133.2 0.1 copy.19
  133.3 0.1 iota_compare_fusion.2
  133.4 0.8 fusion.31
  134.2 0.4 fusion.16
  134.6 0.3 fusion.30
  134.9 0.5 broadcast_multiply_fusion.1
  135.4 1.8 %convolution_convert_fusion.1 = bf16[4,128,512]{2,1,0:T(8,128)(2,1)} fusion(bf16[4,512,512]{2,1,0:T(8,128)(2,1)S(1)} %copy-done, f32[4,128]{1,0:T(4,128)S(1)} %fusion.30, f32[4,128,512]{2,1,0:T(8,128)S(1)} %fusion.16), kind=kOutput, calls=%fused_computation.16 | convolution fusion | flops 269485056 | bytes 3672064 | tf_op jit(solution)/shard_map/rht,rtc->rhc/dot_general | solution.py:22
  137.2 0.0 all-to-all-done.1
  137.2 3.8 %gather_fusion = bf16[128,3584]{1,0:T(8,128)(2,1)S(1)} fusion(bf16[256,3584]{1,0:T(8,128)(2,1)} %bitcast.5, s32[1024]{0:T(1024)S(1)} %pad_clamp_fusion), kind=kCustom, calls=%fused_computation | custom fusion | bytes 1835520 | tf_op jit(solution)/shard_map/gather | solution.py:87
  141.0 0.4 fusion.18
  141.4 0.7 copy.22
  (14 shorter events, 0.0 us)
Async XLA Ops:
  0.6 132.7 %copy-start = (bf16[4,512,512]{2,1,0:T(8,128)(2,1)S(1)}, bf16[4,512,512]{2,1,0:T(8,128)(2,1)}, u32[]{:S(2)}) copy-start(bf16[4,512,512]{2,1,0:T(8,128)(2,1)} %param.17) | copy-start | bytes 6291460
  3.9 59.0 %slice-start = ((s8[7340032]{0:T(1024)(128)(4,1)}), s8[4194304]{0:T(1024)(128)(4,1)S(1)}, s32[]{:S(2)}) async-start(s8[7340032]{0:T(1024)(128)(4,1)} %bitcast.42), calls=%async_computation.2 | async-start | bytes 8388608
  55.4 7.4 %slice-start.1 = ((s8[7340032]{0:T(1024)(128)(4,1)}), s8[3145728]{0:T(1024)(128)(4,1)S(1)}, s32[]{:S(2)}) async-start(s8[7340032]{0:T(1024)(128)(4,1)} %bitcast.42), calls=%async_computation.3 | async-start | bytes 6291456
  66.2 67.0 %copy-start.4 = (f32[16,8]{0,1:T(8,128)S(1)}, f32[16,8]{0,1:T(8,128)}, u32[]{:S(2)}) copy-start(f32[16,8]{0,1:T(8,128)} %param.12) | copy-start | bytes 1540
  66.2 67.1 %copy-start.5 = (s32[4]{0:T(128)S(1)}, s32[4]{0:T(128)}, u32[]{:S(2)}) copy-start(s32[4]{0:T(128)} %param.19) | copy-start | bytes 52
  66.2 67.2 %copy-start.1 = (bf16[4,128,512]{2,1,0:T(8,128)(2,1)S(1)}, bf16[4,128,512]{2,1,0:T(8,128)(2,1)}, u32[]{:S(2)}) copy-start(bf16[4,128,512]{2,1,0:T(8,128)(2,1)} %param.15) | copy-start | bytes 1572868
  66.2 71.0 %all-to-all-start.1 = ((bf16[32,8,3584]{2,1,0:T(8,128)(2,1)}), bf16[32,8,3584]{2,1,0:T(8,128)(2,1)}, u32[]{:S(2)}, u32[]{:S(2)}) async-start(bf16[32,8,3584]{2,1,0:T(8,128)(2,1)} %fusion.9), calls=%async_computation.1 | async-start | bytes 3670016 | tf_op jit(solution)/shard_map/all_to_all | solution.py:76
  69.8 64.4 %copy-start.2 = (bf16[4,64,512]{2,1,0:T(8,128)(2,1)S(1)}, bf16[4,64,512]{2,1,0:T(8,128)(2,1)}, u32[]{:S(2)}) copy-start(bf16[4,64,512]{2,1,0:T(8,128)(2,1)} %param.18) | copy-start | bytes 786436
  69.8 64.4 %copy-start.3 = (bf16[4,64,128]{2,1,0:T(8,128)(2,1)S(1)}, bf16[4,64,128]{2,1,0:T(8,128)(2,1)}, u32[]{:S(2)}) copy-start(bf16[4,64,128]{2,1,0:T(8,128)(2,1)} %param.16) | copy-start | bytes 196612
where the time goes:
time: 142 us
  blocking collectives  115 us (81%)
  matrix products  15.7 us (11%)
  local copies, waits for them, and re-layouts  5.71 us (4%)
  starting transfers between devices  3.57 us (3%)
  other arithmetic  1.48 us (1%)
    psum x1, blocking collectives, per_device(): totals = lax.psum(counts, ('sec', 'dev'))  63.3 us
    all_to_all x1, blocking collectives, per_device(): lax.all_to_all(outgoing, ('sec', 'dev'), split_axis=0, concat_axis=0, til...  51.5 us
    dot_general x1, matrix products, expert_apply(): jnp.dot(flat_rows, w_gate_up[0], preferred_element_type=jnp.float32)  7.4 us
    gather x1, local copies, waits for them, and re-layouts, per_device(): picked = returned.reshape(experts * capacity, model_width)[slot_index]  3.76 us
    all_to_all x1, starting transfers between devices, per_device(): lax.all_to_all(expert_apply(lax.all_to_all(outgoing, ('sec', 'dev'), spli...  3.57 us
    dot_general x1, matrix products, expert_apply(): jnp.dot(activated, w_down[0], preferred_element_type=jnp.float32)  3.34 us
  transfers between devices with their start and end apart: 1, of which 0 were waited for; matrix products, arithmetic and copies ran while one was open for 3% of the time, Pallas kernels for 0%

commit v1 on v0

v1 whole, which is shorter than its diff:
```python
import jax
import jax.numpy as jnp
from jax import lax
from jax.sharding import PartitionSpec as P


def attend(query_latent, query_rope, latent_cache, rope_cache, cache_lengths):
    factor = (query_latent.shape[2] + query_rope.shape[1]) ** (-0.5)
    scores = jnp.einsum(
        "rhc,rtc->rht", query_latent, latent_cache, preferred_element_type=jnp.float32
    )
    scores = scores + jnp.einsum(
        "rph,rpt->rht", query_rope, rope_cache, preferred_element_type=jnp.float32
    )
    scores = scores * factor
    positions = jnp.arange(latent_cache.shape[1], dtype=jnp.int32)
    live_mask = positions[None, None, :] < cache_lengths[:, None, None]
    scores = jnp.where(live_mask, scores, -1e30)
    highest = jnp.max(scores, axis=-1, keepdims=True)
    powers = jnp.exp(scores - highest)
    attention_weights = (powers / jnp.sum(powers, axis=-1, keepdims=True)).astype(jnp.bfloat16)
    result = jnp.einsum(
        "rht,rtc->rhc", attention_weights, latent_cache, preferred_element_type=jnp.float32
    )
    return result.astype(jnp.bfloat16)


def per_device(
    hidden,
    expert_ids,
    route_weights,
    w_gate_up,
    w_down,
    query_latent,
    query_rope,
    latent_cache,
    rope_cache,
    cache_lengths,
):
    axes = ("sec", "dev")
    row_count, model_width = hidden.shape
    top_count = expert_ids.shape[1]
    experts = lax.axis_size("sec") * lax.axis_size("dev")
    capacity = 2 * row_count * top_count // experts
    me = lax.axis_index("sec") * lax.axis_size("dev") + lax.axis_index("dev")
    routes = jnp.concatenate([expert_ids.astype(jnp.float32), route_weights], axis=1)
    routes = lax.all_gather(routes, axes, axis=0, tiled=True)
    rows = lax.all_gather(hidden, axes, axis=0, tiled=True)
    all_ids = routes[:, :top_count].astype(jnp.int32)
    hit = all_ids == me
    weight = jnp.sum(jnp.where(hit, routes[:, top_count:], 0.0), axis=1)
    chosen = jnp.any(hit, axis=1).astype(jnp.int32).reshape(experts, row_count)
    rank = jnp.cumsum(chosen, axis=1) - chosen
    slot = jnp.where(chosen > 0, jnp.arange(experts)[:, None] * capacity + rank, -1).reshape(-1)
    placer = (jnp.arange(experts * capacity)[:, None] == slot[None, :]).astype(jnp.bfloat16)
    received = jnp.dot(placer, rows, preferred_element_type=jnp.float32).astype(jnp.bfloat16)
    projected = jnp.dot(received, w_gate_up[0], preferred_element_type=jnp.float32)
    hidden_units = w_down.shape[1]
    activated = (jax.nn.silu(projected[:, :hidden_units]) * projected[:, hidden_units:]).astype(
        jnp.bfloat16
    )
    produced = jnp.dot(activated, w_down[0], preferred_element_type=jnp.float32).astype(
        jnp.bfloat16
    )
    spread = lax.dot_general(
        placer, produced, (((0,), (0,)), ((), ())), preferred_element_type=jnp.float32
    )
    partial = (spread * weight[:, None]).astype(jnp.bfloat16)
    moe_out = lax.psum_scatter(partial, axes, scatter_dimension=0, tiled=True)
    expert_range = jnp.arange(experts, dtype=jnp.int32)
    counts = jnp.sum((all_ids.reshape(-1)[:, None] == expert_range).astype(jnp.float32), axis=0)
    expert_load = counts / float(row_count * top_count)
    attention_out = attend(query_latent, query_rope, latent_cache, rope_cache, cache_lengths)
    return (moe_out, expert_load, attention_out)


def solution(mesh):
    return jax.shard_map(
        per_device,
        mesh=mesh,
        in_specs=(
            P(("sec", "dev"), None),
            P(("sec", "dev"), None),
            P(("sec", "dev"), None),
            P(("sec", "dev"), None, None),
            P(("sec", "dev"), None, None),
            P(("sec", "dev"), None, None),
            P(("sec", "dev"), None, None),
            P(("sec", "dev"), None, None),
            P(("sec", "dev"), None, None),
            P(("sec", "dev")),
        ),
        out_specs=(P(("sec", "dev"), None), P(), P(("sec", "dev"), None, None)),
        check_vma=False,
    )
```

time: 142 us -> 240 us (1.69)
  waiting for transfers between devices: 0.01 us -> 154 us
  blocking collectives: 115 us -> 44.8 us
  between operations: 0.82 us -> 14.1 us
  matrix products: 15.7 us -> 22.8 us
  local copies, waits for them, and re-layouts: 5.71 us -> 1.18 us
  starting transfers between devices: 3.57 us -> 0.08 us
    reduce_scatter x0 -> x1, waiting for transfers between devices: none -> 134 us  [per_device(): moe_out = lax.psum_scatter(partial, axes, scatter_dimension=0, tiled=True)]
    psum x1 -> x0, blocking collectives: 63.3 us -> none  [per_device(): totals = lax.psum(counts, ('sec', 'dev'))]
    all_to_all x1 -> x0, blocking collectives: 51.5 us -> none  [per_device(): lax.all_to_all(outgoing, ('sec', 'dev'), split_axis=0, concat_axis=0, til...]
    all_gather x0 -> x1, blocking collectives: none -> 44.8 us  [per_device(): routes = lax.all_gather(routes, axes, axis=0, tiled=True)]
    all_gather x0 -> x1, waiting for transfers between devices: none -> 19 us  [per_device(): rows = lax.all_gather(hidden, axes, axis=0, tiled=True)]
    dot_general x4 -> x2, matrix products: 12.7 us -> 19.8 us  [the longest x1 11.2 us: per_device(): jnp.dot(received, w_gate_up[0], preferred_element_type=jnp.float32)]
    gather x1 -> x0, local copies, waits for them, and re-layouts: 3.76 us -> none  [per_device(): picked = returned.reshape(experts * capacity, model_width)[slot_index]]
    all_to_all x1 -> x0, starting transfers between devices: 3.57 us -> none  [per_device(): lax.all_to_all(expert_apply(lax.all_to_all(outgoing, ('sec', 'dev'), spli...]
  transfers between devices with their start and end apart: 1 -> 2, of which waited for: 0 -> 2; matrix products, arithmetic and copies ran while one was open for 3% -> 3% of each run, Pallas kernels for 0% -> 0%
where the time goes in v1:
time: 240 us
  waiting for transfers between devices  154 us (64%)
  blocking collectives  44.8 us (19%)
  matrix products  22.8 us (10%)
  between operations  14.1 us (6%)
  other arithmetic  3.03 us (1%)
    reduce_scatter x1, waiting for transfers between devices, per_device(): moe_out = lax.psum_scatter(partial, axes, scatter_dimension=0, tiled=True)  134 us
    all_gather x1, blocking collectives, per_device(): routes = lax.all_gather(routes, axes, axis=0, tiled=True)  44.8 us
    all_gather x1, waiting for transfers between devices, per_device(): rows = lax.all_gather(hidden, axes, axis=0, tiled=True)  19 us
    dot_general x1, matrix products, per_device(): jnp.dot(received, w_gate_up[0], preferred_element_type=jnp.float32)  11.2 us
    dot_general x1, matrix products, per_device(): lax.dot_general(placer, produced, (((0,), (0,)), ((), ())), preferred_ele...  8.59 us
  transfers between devices with their start and end apart: 2, of which 2 were waited for; matrix products, arithmetic and copies ran while one was open for 3% of the time, Pallas kernels for 0%

profile of v1, /device:TPU:0, one launch (start us, length us, event | category | flops | bytes accessed | tf_op | source)
XLA Modules:
  0.0 240.2 jit_solution(11522464038882184178)
XLA Ops:
  7.2 0.0 copy-start
  7.2 0.0 all-gather.2.cloned.1.call-start
  7.2 0.7 all-gather.2.cloned.1.call-update
  7.9 0.0 reduce-scatter.2.cloned.1.call-start
  8.0 0.7 convert_element_type.41
  8.7 0.7 pad_maximum_fusion
  9.3 0.1 copy.18
  9.4 0.1 add.27
  9.5 0.1 add.28
  9.6 44.8 %all_gather.6 = f32[512,16]{1,0:T(8,128)S(1)} all-gather(f32[16,16]{1,0:T(8,128)S(1)} %copy.18), channel_id=1, replica_groups=mesh['sec'=4,'dev'=8] {'sec','dev'}, dimensions={0}, use_global_device_ids=true | all-gather | bytes 33792 | tf_op jit(solution)/shard_map/all_gather | solution.py:47
  54.4 0.2 fusion.27
  54.6 0.1 reshape.57
  54.6 0.2 reduce_window_sum.13
  54.8 0.1 reduce_window_sum.14
  54.9 0.2 slice_convert_fusion
  55.1 19.0 %all-gather.2.cloned.1.call-done = bf16[512,3584]{1,0:T(8,128)(2,1)} async-done(((bf16[16,3584]{1,0:T(8,128)(2,1)}), bf16[512,3584]{1,0:T(8,128)(2,1)}) %all-gather.2.cloned.1.call-update) | async-done | bytes 3670032 | tf_op jit(solution)/shard_map/all_gather | solution.py:48
  74.2 11.2 %fusion.1 = f32[256,2048]{1,0:T(8,128)} fusion(bf16[1,3584,2048]{2,1,0:T(8,128)(2,1)} %param.13, bf16[512,3584]{1,0:T(8,128)(2,1)} %all-gather.2.cloned.1.call-done, s32[512]{0:T(512)S(1)} %add_select_fusion), kind=kOutput, calls=%fused_computation.1 | convolution fusion | flops 4698669056 | bytes 20449280 | tf_op jit(solution)/shard_map/dot_general | solution.py:57
  85.4 8.6 %multiply_convert_fusion = bf16[512,3584]{1,0:T(8,128)(2,1)} fusion(f32[512]{0:T(512)S(1)} %get-tuple-element.6, bf16[1,1024,3584]{2,1,0:T(8,128)(2,1)} %param.14, f32[256,2048]{1,0:T(8,128)} %fusion.1, s32[512]{0:T(512)S(1)} %add_select_fusion), kind=kOutput, calls=%fused_computation.5 | convolution fusion | flops 2824863744 | bytes 13111296 | tf_op jit(solution)/shard_map/dot_general | solution.py:65
  94.0 0.0 reduce-scatter.2.cloned.1.call-update
  94.0 0.1 eq.39
  94.2 0.2 convert_reduce_fusion
  94.3 0.3 copy-done.4
  94.6 0.1 iota_compare_fusion.5
  94.7 0.0 copy-done
  94.7 0.3 copy-done.1
  95.0 0.8 fusion.29
  95.8 0.0 copy-done.2
  95.8 0.4 fusion.11
  96.2 0.3 fusion.28
  96.5 0.5 broadcast_multiply_fusion
  97.0 1.8 convolution_convert_fusion.1
  98.9 134.4 %reduce-scatter.2.cloned.1.call-done = bf16[16,3584]{1,0:T(8,128)(2,1)} async-done(((bf16[512,3584]{1,0:T(8,128)(2,1)}), bf16[16,3584]{1,0:T(8,128)(2,1)}) %reduce-scatter.2.cloned.1.call-update) | async-done | bytes 114704 | tf_op jit(solution)/shard_map/reduce_scatter | solution.py:69
  (8 shorter events, 0.0 us)
Async XLA Ops:
  7.2 87.5 %copy-start = (bf16[4,512,512]{2,1,0:T(8,128)(2,1)S(1)}, bf16[4,512,512]{2,1,0:T(8,128)(2,1)}, u32[]{:S(2)}) copy-start(bf16[4,512,512]{2,1,0:T(8,128)(2,1)} %param.17) | copy-start | bytes 6291460
  7.2 67.0 %all-gather.2.cloned.1.call-start = ((), (), s32[]{:S(2)}) async-start(), calls=%async_computation.1 | async-start | bytes 3784704 | tf_op jit(solution)/shard_map/all_gather | solution.py:48
  7.9 225.4 %reduce-scatter.2.cloned.1.call-start = ((), (), s32[]{:S(2)}) async-start(), calls=%async_computation.2 | async-start | bytes 3784704 | tf_op jit(solution)/shard_map/reduce_scatter | solution.py:69
  94.0 0.7 copy-start.4
  94.0 1.1 copy-start.1
  94.0 1.9 copy-start.2
  94.0 1.9 copy-start.3
Sparse Core Ops, SparseCore 0:
  10.9 63.2 all-gather.1
  94.1 139.1 reduce-scatter.1

commit v2 on v1

v2 whole, which is shorter than its diff:
```python
import functools

import jax
import jax.numpy as jnp
from jax import lax
from jax.experimental import pallas as pl
from jax.experimental.pallas import tpu as pltpu
from jax.sharding import PartitionSpec as P

WIDTH = 512
MESH = pl.DeviceIdType.MESH
F32 = jnp.float32
BF16 = jnp.bfloat16


def kernel(
    slots_per,
    x_ref,
    table_ref,
    lengths_ref,
    gate_up_hbm,
    down_hbm,
    ql_hbm,
    qr_hbm,
    lat_hbm,
    rope_hbm,
    out_ref,
    load_ref,
    att_ref,
    rows_buf,
    table_buf,
    gate_up,
    down,
    ql,
    qr,
    lat,
    rope,
    projected,
    activated,
    placer,
    placer_t,
    weight,
    from_sib,
    from_first,
    from_second,
    from_line,
    local_sem,
    line_send,
    line_recv,
    hop_send,
    hop_recv,
    back_send,
    back_recv,
    back_line_send,
    back_line_recv,
):
    chunks = rows_buf.shape[0]
    line = rows_buf.shape[3]
    rows = x_ref.shape[0]
    tokens = 2 * 4 * line * rows
    units = down.shape[0]
    s = lax.axis_index("sec")
    d = lax.axis_index("dev")
    m = d // 2
    k = lax.rem(d, 2)
    experts = 8 * line
    me = s * (2 * line) + d

    def xor(j):
        low = lax.rem(s, 2)
        high = s // 2
        if j & 1:
            low = 1 - low
        if j & 2:
            high = 1 - high
        return high * 2 + low

    secs = [s, xor(1), xor(2), xor(3)]
    sib = (s, m * 2 + (1 - k))
    across = {1: (secs[1], d), 2: (secs[2], d)}

    def on_line(step):
        return (s, lax.rem(m + step, line) * 2 + k)

    local = []

    def fetch(src, dst):
        copy = pltpu.make_async_copy(src, dst, local_sem.at[len(local)])
        copy.start()
        local.append(copy)
        return copy

    partners = [sib, across[1], across[2]] + [on_line(i) for i in range(1, line)]
    barrier = pltpu.get_barrier_semaphore()
    for partner in partners:
        pl.semaphore_signal(barrier, inc=1, device_id=partner, device_id_type=MESH)
    att_copies = [fetch(a, b) for a, b in ((ql_hbm, ql), (qr_hbm, qr), (lat_hbm, lat), (rope_hbm, rope))]
    gate_copies = [
        fetch(gate_up_hbm.at[0, pl.ds(c * WIDTH, WIDTH)], gate_up.at[pl.ds(c * WIDTH, WIDTH)])
        for c in range(chunks)
    ]
    down_copy = fetch(down_hbm.at[0], down)

    table_buf[k, s, m] = table_ref[...]
    for c in range(chunks):
        rows_buf[c, k, s, m] = x_ref[:, c * WIDTH : (c + 1) * WIDTH]
    pl.semaphore_wait(barrier, len(partners))

    started = []

    def send(src, dst, send_sem, recv_sem, device):
        copy = pltpu.make_async_remote_copy(
            src_ref=src, dst_ref=dst, send_sem=send_sem, recv_sem=recv_sem,
            device_id=device, device_id_type=MESH,
        )
        copy.start()
        started.append(copy)
        return copy

    pieces = [table_buf] + [rows_buf.at[c] for c in range(chunks)]
    line_copies, own, fwd, sibs = {}, {}, {}, {}
    for i, buf in enumerate(pieces):
        line_copies[i] = [
            send(buf.at[k, s, m], buf.at[k, s, m], line_send.at[i, j - 1], line_recv.at[i, j - 1], on_line(j))
            for j in range(1, line)
        ]

    def hop(i, group, kind, device):
        buf = pieces[i]
        return send(buf.at[k, group], buf.at[k, group], hop_send.at[i, kind], hop_recv.at[i, kind], device)

    def stage_own(i):
        for copy in line_copies[i]:
            copy.wait_recv()
        own[i] = [hop(i, s, 0, across[1]), hop(i, s, 1, across[2])]
        sibs[i] = [hop(i, s, 3, sib)]

    def stage_cross(i):
        own[i][i % 2].wait_recv()
        fwd[i] = hop(i, secs[1 + i % 2], 2, across[2 - i % 2])
        sibs[i].append(hop(i, secs[1 + i % 2], 4, sib))
        own[i][1 - i % 2].wait_recv()
        sibs[i].append(hop(i, secs[2 - i % 2], 5, sib))

    def stage_diagonal(i):
        fwd[i].wait_recv()
        sibs[i].append(hop(i, secs[3], 6, sib))

    def routing():
        lanes = table_buf.shape[-1]
        part = 8 * rows
        table = table_buf[...].reshape(tokens, lanes)
        chosen = (table > 0.0).astype(F32)
        load_ref[...] = jnp.sum(chosen, axis=0, keepdims=True) / float(tokens * slots_per[1] // experts)
        lane = lax.broadcasted_iota(jnp.int32, (tokens, lanes), 1)
        mine = jnp.sum(jnp.where(lane == me, table, 0.0), axis=1, keepdims=True)
        weight[...] = mine
        r = lax.broadcasted_iota(jnp.int32, (part, part), 0)
        q = lax.broadcasted_iota(jnp.int32, (part, part), 1)
        before = jnp.where((r // rows == q // rows) & (q < r), 1.0, 0.0).astype(BF16)
        for b in range(tokens // part):
            cut = slice(b * part, (b + 1) * part)
            hit = (mine[cut] > 0.0).astype(F32)
            rank = jnp.dot(before, jnp.broadcast_to(hit, (part, 128)).astype(BF16), preferred_element_type=F32)[:, :1]
            block = lax.broadcasted_iota(jnp.int32, (part, 1), 0) // rows + b * 8
            slot = jnp.where(hit > 0.0, block.astype(F32) * float(slots_per[0]) + rank, -1.0)
            spots = lax.broadcasted_iota(jnp.int32, (part, experts * slots_per[0]), 1).astype(F32)
            picks = jnp.where(spots == slot, 1.0, 0.0)
            placer_t[cut, :] = picks.astype(BF16)
            placer[:, cut] = picks.T.astype(BF16)

    def attend(r):
        scores = lax.dot_general(ql[r], lat[r], (((1,), (1,)), ((), ())), preferred_element_type=F32)
        scores = scores + lax.dot_general(qr[r], rope[r], (((0,), (0,)), ((), ())), preferred_element_type=F32)
        scores = scores * ((ql.shape[2] + qr.shape[1]) ** -0.5)
        positions = lax.broadcasted_iota(jnp.int32, scores.shape, 1)
        scores = jnp.where(positions < lengths_ref[r], scores, -1e30)
        powers = jnp.exp(scores - jnp.max(scores, axis=-1, keepdims=True))
        weights = (powers / jnp.sum(powers, axis=-1, keepdims=True)).astype(BF16)
        att_ref[r] = jnp.dot(weights, lat[r], preferred_element_type=F32).astype(BF16)

    def stage_up(i):
        for copy in sibs[i]:
            copy.wait_recv()
        if i == 0:
            routing()
            return
        c = i - 1
        gate_copies[c].wait()
        received = jnp.dot(
            placer[...], rows_buf[c].reshape(tokens, WIDTH), preferred_element_type=F32
        ).astype(BF16)

        @pl.loop(0, 2 * units // 512)
        def _(t):
            cols = pl.ds(pl.multiple_of(t * 512, 512), 512)
            part = jnp.dot(received, gate_up[pl.ds(c * WIDTH, WIDTH), cols], preferred_element_type=F32)
            if c == 0:
                projected[:, cols] = part
            else:
                projected[:, cols] += part

    count = chunks + 1
    for copy in att_copies:
        copy.wait()
    att_rows = ql.shape[0]
    attended = 0
    for i in range(count + 3):
        if i < count:
            stage_own(i)
        if 0 <= i - 1 < count:
            stage_cross(i - 1)
        if 0 <= i - 2 < count:
            stage_diagonal(i - 2)
        if attended < att_rows:
            attend(attended)
            attended += 1
        if 0 <= i - 3 < count:
            stage_up(i - 3)
    for r in range(attended, att_rows):
        attend(r)
    for copy in started:
        copy.wait_send()

    for t in range(0, units, 256):
        gate = projected[:, t : t + 256]
        up = projected[:, units + t : units + t + 256]
        activated[:, t : t + 256] = (gate / (1.0 + jnp.exp(-gate)) * up).astype(BF16)
    down_copy.wait()

    started.clear()
    sib_in, first_in, second_in, line_in = {}, {}, {}, {}

    def stage_down(c):
        produced = jnp.dot(
            activated[...], down[:, c * WIDTH : (c + 1) * WIDTH], preferred_element_type=F32
        ).astype(BF16)
        half = tokens // 2
        for side in (0, 1):
            group = (1 - k) if side == 0 else k
            start = pl.multiple_of(group * half, half)
            spread = jnp.dot(placer_t[pl.ds(start, half), :], produced, preferred_element_type=F32)
            spread = spread * weight[pl.ds(start, half), :]
            rows_buf[c, group] = spread.astype(BF16).reshape(4, line, rows, WIDTH)
            if side == 0:
                sib_in[c] = send(rows_buf.at[c, group], from_sib.at[c], back_send.at[c, 0], back_recv.at[c, 0], sib)

    def add(c, group, value):
        rows_buf[c, k, group] = (rows_buf[c, k, group].astype(F32) + value.astype(F32)).astype(BF16)

    def stage_first(c):
        sib_in[c].wait_recv()
        one = 1 + c % 2
        for j in (one, 3, 3 - one, 0):
            add(c, secs[j], from_sib[c, secs[j]])
            if j == one:
                a = send(rows_buf.at[c, k, secs[one]], from_first.at[c, 0], back_send.at[c, 1], back_recv.at[c, 1], across[one])
            if j == 3:
                b = send(rows_buf.at[c, k, secs[3]], from_first.at[c, 1], back_send.at[c, 2], back_recv.at[c, 2], across[one])
        first_in[c] = [a, b]

    def stage_second(c):
        two = 2 - c % 2
        for copy in first_in[c]:
            copy.wait_recv()
        add(c, secs[two], from_first[c, 1])
        second_in[c] = send(rows_buf.at[c, k, secs[two]], from_second.at[c], back_send.at[c, 3], back_recv.at[c, 3], across[two])
        add(c, s, from_first[c, 0])

    def stage_line(c):
        second_in[c].wait_recv()
        add(c, s, from_second[c])
        line_in[c] = [
            send(
                rows_buf.at[c, k, s, lax.rem(m + j, line)], from_line.at[c, j - 1],
                back_line_send.at[c, j - 1], back_line_recv.at[c, j - 1], on_line(j),
            )
            for j in range(1, line)
        ]

    def stage_out(c):
        total = rows_buf[c, k, s, m].astype(F32)
        for j, copy in enumerate(line_in[c]):
            copy.wait_recv()
            total = total + from_line[c, j].astype(F32)
        out_ref[:, c * WIDTH : (c + 1) * WIDTH] = total.astype(BF16)

    for i in range(chunks + 4):
        for lag, stage in enumerate((stage_down, stage_first, stage_second, stage_line, stage_out)):
            if 0 <= i - lag < chunks:
                stage(i - lag)
    for copy in started:
        copy.wait_send()


def per_device(
    hidden,
    expert_ids,
    route_weights,
    w_gate_up,
    w_down,
    query_latent,
    query_rope,
    latent_cache,
    rope_cache,
    cache_lengths,
):
    rows, model_width = hidden.shape
    top_count = expert_ids.shape[1]
    members = lax.axis_size("dev")
    experts = lax.axis_size("sec") * members
    line = members // 2
    capacity = 2 * rows * top_count // experts
    slots = experts * capacity
    tokens = experts * rows
    units = w_down.shape[1]
    lanes = -(-experts // 128) * 128
    chunks = model_width // WIDTH
    pieces = chunks + 1
    att_rows = query_latent.shape[0]
    hits = expert_ids[:, :, None] == jnp.arange(lanes, dtype=jnp.int32)
    table = jnp.sum(jnp.where(hits, route_weights[:, :, None], 0.0), axis=1)
    vmem = pl.BlockSpec(memory_space=pltpu.VMEM)
    smem = pl.BlockSpec(memory_space=pltpu.SMEM)
    hbm = pl.BlockSpec(memory_space=pl.ANY)
    dma = pltpu.SemaphoreType.DMA
    moe_out, load, attention_out = pl.pallas_call(
        functools.partial(kernel, (capacity, top_count)),
        out_shape=(
            jax.ShapeDtypeStruct((rows, model_width), BF16),
            jax.ShapeDtypeStruct((1, lanes), F32),
            jax.ShapeDtypeStruct(query_latent.shape, BF16),
        ),
        in_specs=[vmem, vmem, smem, hbm, hbm, hbm, hbm, hbm, hbm],
        out_specs=(vmem, vmem, vmem),
        scratch_shapes=[
            pltpu.VMEM((chunks, 2, 4, line, rows, WIDTH), BF16),
            pltpu.VMEM((2, 4, line, rows, lanes), F32),
            pltpu.VMEM(w_gate_up.shape[1:], BF16),
            pltpu.VMEM(w_down.shape[1:], BF16),
            pltpu.VMEM(query_latent.shape, BF16),
            pltpu.VMEM(query_rope.shape, BF16),
            pltpu.VMEM(latent_cache.shape, BF16),
            pltpu.VMEM(rope_cache.shape, BF16),
            pltpu.VMEM((slots, 2 * units), F32),
            pltpu.VMEM((slots, units), BF16),
            pltpu.VMEM((slots, tokens), BF16),
            pltpu.VMEM((tokens, slots), BF16),
            pltpu.VMEM((tokens, 1), F32),
            pltpu.VMEM((chunks, 4, line, rows, WIDTH), BF16),
            pltpu.VMEM((chunks, 2, line, rows, WIDTH), BF16),
            pltpu.VMEM((chunks, line, rows, WIDTH), BF16),
            pltpu.VMEM((chunks, line - 1, rows, WIDTH), BF16),
            dma((chunks + 5,)),
            dma((pieces, line - 1)),
            dma((pieces, line - 1)),
            dma((pieces, 7)),
            dma((pieces, 7)),
            dma((chunks, 4)),
            dma((chunks, 4)),
            dma((chunks, line - 1)),
            dma((chunks, line - 1)),
        ],
        compiler_params=pltpu.CompilerParams(
            collective_id=0, has_side_effects=True, vmem_limit_bytes=62 * 1024 * 1024
        ),
        name="experts_and_attention",
    )(
        hidden, table, cache_lengths, w_gate_up, w_down,
        query_latent, query_rope, latent_cache, rope_cache,
    )
    return (moe_out, load[0, :experts], attention_out)


def solution(mesh):
    return jax.shard_map(
        per_device,
        mesh=mesh,
        in_specs=(
            P(("sec", "dev"), None),
            P(("sec", "dev"), None),
            P(("sec", "dev"), None),
            P(("sec", "dev"), None, None),
            P(("sec", "dev"), None, None),
            P(("sec", "dev"), None, None),
            P(("sec", "dev"), None, None),
            P(("sec", "dev"), None, None),
            P(("sec", "dev"), None, None),
            P(("sec", "dev")),
        ),
        out_specs=(P(("sec", "dev"), None), P(), P(("sec", "dev"), None, None)),
        check_vma=False,
    )
```

time: 240 us -> 83.1 us (0.35)
  waiting for transfers between devices: 154 us -> 0 us
  Pallas kernels: 0 us -> 75.4 us
  blocking collectives: 44.8 us -> 0 us
  matrix products: 22.8 us -> 0 us
  between operations: 14.1 us -> 0.64 us
  local copies, waits for them, and re-layouts: 1.18 us -> 6.04 us
    reduce_scatter x1 -> x0, waiting for transfers between devices: 134 us -> none  [per_device(): moe_out = lax.psum_scatter(partial, axes, scatter_dimension=0, tiled=True)]
    pallas_call x0 -> x1, Pallas kernels: none -> 75.4 us  [per_device(): pl.pallas_call(functools.partial(kernel, (capacity, top_count)), out_shap...]
    all_gather x1 -> x0, blocking collectives: 44.8 us -> none  [per_device(): routes = lax.all_gather(routes, axes, axis=0, tiled=True)]
    dot_general x5 -> x0, matrix products: 22.8 us -> none  [the longest x1 11.2 us: per_device(): jnp.dot(received, w_gate_up[0], preferred_element_type=jnp.float32)]
    all_gather x1 -> x0, waiting for transfers between devices: 19 us -> none  [per_device(): rows = lax.all_gather(hidden, axes, axis=0, tiled=True)]
    unnamed x10 -> x4, local copies, waits for them, and re-layouts: 0.64 us -> 4.93 us
  transfers between devices with their start and end apart: 2 -> 0, of which waited for: 2 -> 0; matrix products, arithmetic and copies ran while one was open for 3% -> 0% of each run, Pallas kernels for 0% -> 0%
where the time goes in v2:
time: 83.1 us; the launch traced here: 82.8 us
  Pallas kernels  75.4 us (91%)
  local copies, waits for them, and re-layouts  6.04 us (7%)
    pallas_call x1, Pallas kernels, per_device(): pl.pallas_call(functools.partial(kernel, (capacity, top_count)), out_shap...  75.4 us
    unnamed x4, local copies, waits for them, and re-layouts  4.93 us

profile of v2, /device:TPU:0, one launch (start us, length us, event | category | flops | bytes accessed | tf_op | source)
XLA Modules:
  0.0 82.8 jit_solution(2437853009310120993)
XLA Ops:
  0.6 0.8 copy.15
  1.4 0.8 copy.16
  2.1 0.7 select_reduce_fusion.table_ref
  2.9 75.4 %experts_and_attention.1 = (bf16[16,3584]{1,0:T(8,128)(2,1)}, f32[1,128]{1,0:T(1,128)}, bf16[4,128,512]{2,1,0:T(8,128)(2,1)}) custom-call(bf16[16,3584]{1,0:T(8,128)(2,1)} %x_ref.1, f32[16,128]{1,0:T(8,128)} %select_reduce_fusion.table_ref, s32[4]{0:T(128)} %lengths_ref.1, bf16[1,3584,2048]{2,1,0:T(8,128)(2,1)} %gate_up_hbm.1, ...), custom_call_target="tpu_custom_call" | custom-call | tf_op jit(solution)/shard_map/experts_and_attention/pallas_call | solution.py:327
  78.3 1.1 %slice_bitcast_fusion = f32[32]{0:T(128)} fusion(f32[1,128]{1,0:T(1,128)} %get-tuple-element.7), kind=kLoop, calls=%fused_computation.2 | loop fusion | bytes 256 | tf_op jit(solution)/shard_map/squeeze | solution.py:372
  79.4 1.6 %copy.19 = bf16[16,3584]{1,0:T(8,128)(2,1)} copy(bf16[16,3584]{1,0:T(8,128)(2,1)} %get-tuple-element.12) | data formatting | bytes 229376
  80.9 1.9 %copy.20 = bf16[4,128,512]{2,1,0:T(8,128)(2,1)} copy(bf16[4,128,512]{2,1,0:T(8,128)(2,1)} %get-tuple-element.14) | data formatting | bytes 1048576

commit v3 on v2

--- a/solution.py
+++ b/solution.py
@@ -7,7 +7,7 @@
 from jax.experimental.pallas import tpu as pltpu
 from jax.sharding import PartitionSpec as P
 
-WIDTH = 512
+WIDTH = 256
 MESH = pl.DeviceIdType.MESH
 F32 = jnp.float32
 BF16 = jnp.bfloat16
@@ -16,7 +16,8 @@
 def kernel(
     slots_per,
     x_ref,
-    table_ref,
+    ids_ref,
+    route_ref,
     lengths_ref,
     gate_up_hbm,
     down_hbm,
@@ -95,13 +96,20 @@
     for partner in partners:
         pl.semaphore_signal(barrier, inc=1, device_id=partner, device_id_type=MESH)
     att_copies = [fetch(a, b) for a, b in ((ql_hbm, ql), (qr_hbm, qr), (lat_hbm, lat), (rope_hbm, rope))]
-    gate_copies = [
-        fetch(gate_up_hbm.at[0, pl.ds(c * WIDTH, WIDTH)], gate_up.at[pl.ds(c * WIDTH, WIDTH)])
-        for c in range(chunks)
-    ]
-    down_copy = fetch(down_hbm.at[0], down)
-
-    table_buf[k, s, m] = table_ref[...]
+    gate_copies = []
+
+    def fetch_gate():
+        cut = pl.ds(len(gate_copies) * WIDTH, WIDTH)
+        gate_copies.append(fetch(gate_up_hbm.at[0, cut], gate_up.at[cut]))
+
+    for _ in range(2):
+        fetch_gate()
+    lanes = table_buf.shape[-1]
+    names = lax.broadcasted_iota(jnp.int32, (lanes, rows), 0)
+    table = jnp.zeros((lanes, rows), F32)
+    for j in range(ids_ref.shape[0]):
+        table = table + jnp.where(names == ids_ref[j : j + 1, :], route_ref[j : j + 1, :], 0.0)
+    table_buf[k, s, m] = table.T
     for c in range(chunks):
         rows_buf[c, k, s, m] = x_ref[:, c * WIDTH : (c + 1) * WIDTH]
     pl.semaphore_wait(barrier, len(partners))
@@ -147,11 +155,11 @@
         sibs[i].append(hop(i, secs[3], 6, sib))
 
     def routing():
-        lanes = table_buf.shape[-1]
         part = 8 * rows
         table = table_buf[...].reshape(tokens, lanes)
         chosen = (table > 0.0).astype(F32)
-        load_ref[...] = jnp.sum(chosen, axis=0, keepdims=True) / float(tokens * slots_per[1] // experts)
+        load = jnp.sum(chosen, axis=0, keepdims=True) / float(tokens * slots_per[1] // experts)
+        load_ref[...] = load[:, :experts]
         lane = lax.broadcasted_iota(jnp.int32, (tokens, lanes), 1)
         mine = jnp.sum(jnp.where(lane == me, table, 0.0), axis=1, keepdims=True)
         weight[...] = mine
@@ -205,18 +213,22 @@
         copy.wait()
     att_rows = ql.shape[0]
     attended = 0
-    for i in range(count + 3):
+    for i in range(count + 5):
         if i < count:
             stage_own(i)
-        if 0 <= i - 1 < count:
-            stage_cross(i - 1)
         if 0 <= i - 2 < count:
-            stage_diagonal(i - 2)
-        if attended < att_rows:
+            stage_cross(i - 2)
+        if 0 <= i - 4 < count:
+            stage_diagonal(i - 4)
+        if len(gate_copies) < chunks:
+            fetch_gate()
+        if i == 4:
+            down_copy = fetch(down_hbm.at[0], down)
+        if attended < att_rows and i >= 1:
             attend(attended)
             attended += 1
-        if 0 <= i - 3 < count:
-            stage_up(i - 3)
+        if 0 <= i - 5 < count:
+            stage_up(i - 5)
     for r in range(attended, att_rows):
         attend(r)
     for copy in started:
@@ -285,8 +297,9 @@
             total = total + from_line[c, j].astype(F32)
         out_ref[:, c * WIDTH : (c + 1) * WIDTH] = total.astype(BF16)
 
-    for i in range(chunks + 4):
-        for lag, stage in enumerate((stage_down, stage_first, stage_second, stage_line, stage_out)):
+    schedule = ((0, stage_down), (1, stage_first), (3, stage_second), (5, stage_line), (7, stage_out))
+    for i in range(chunks + 7):
+        for lag, stage in schedule:
             if 0 <= i - lag < chunks:
                 stage(i - lag)
     for copy in started:
@@ -318,8 +331,6 @@
     chunks = model_width // WIDTH
     pieces = chunks + 1
     att_rows = query_latent.shape[0]
-    hits = expert_ids[:, :, None] == jnp.arange(lanes, dtype=jnp.int32)
-    table = jnp.sum(jnp.where(hits, route_weights[:, :, None], 0.0), axis=1)
     vmem = pl.BlockSpec(memory_space=pltpu.VMEM)
     smem = pl.BlockSpec(memory_space=pltpu.SMEM)
     hbm = pl.BlockSpec(memory_space=pl.ANY)
@@ -328,10 +339,10 @@
         functools.partial(kernel, (capacity, top_count)),
         out_shape=(
             jax.ShapeDtypeStruct((rows, model_width), BF16),
-            jax.ShapeDtypeStruct((1, lanes), F32),
+            jax.ShapeDtypeStruct((1, experts), F32),
             jax.ShapeDtypeStruct(query_latent.shape, BF16),
         ),
-        in_specs=[vmem, vmem, smem, hbm, hbm, hbm, hbm, hbm, hbm],
+        in_specs=[vmem, vmem, vmem, smem, hbm, hbm, hbm, hbm, hbm, hbm],
         out_specs=(vmem, vmem, vmem),
         scratch_shapes=[
             pltpu.VMEM((chunks, 2, 4, line, rows, WIDTH), BF16),
@@ -366,10 +377,10 @@
         ),
         name="experts_and_attention",
     )(
-        hidden, table, cache_lengths, w_gate_up, w_down,
+        hidden, expert_ids.T, route_weights.T, cache_lengths, w_gate_up, w_down,
         query_latent, query_rope, latent_cache, rope_cache,
     )
-    return (moe_out, load[0, :experts], attention_out)
+    return (moe_out, load.reshape(experts), attention_out)
 
 
 def solution(mesh):

time: 83.1 us -> 83.8 us (level)
  Pallas kernels: 75.4 us -> 78.4 us
  local copies, waits for them, and re-layouts: 6.04 us -> 4.54 us
    pallas_call x1, Pallas kernels: 75.4 us -> 78.4 us  [per_device(): pl.pallas_call(functools.partial(kernel, (capacity, top_count)), out_shap...]
    squeeze x1 -> x0, local copies, waits for them, and re-layouts: 1.11 us -> none  [per_device(): return (moe_out, load[0, :experts], attention_out)]
    unnamed x4 -> x3, local copies, waits for them, and re-layouts: 4.93 us -> 4.54 us
where the time goes in v3:
time: 83.8 us; the launch traced here: 83.6 us
  Pallas kernels  78.4 us (94%)
  local copies, waits for them, and re-layouts  4.54 us (5%)
    pallas_call x1, Pallas kernels, per_device(): pl.pallas_call(functools.partial(kernel, (capacity, top_count)), out_shap...  78.4 us
    unnamed x3, local copies, waits for them, and re-layouts  4.54 us

profile of v3, /device:TPU:0, one launch (start us, length us, event | category | flops | bytes accessed | tf_op | source)
XLA Modules:
  0.0 83.6 jit_solution(4732658927207657823)
XLA Ops:
  0.6 78.4 %experts_and_attention.1 = (bf16[16,3584]{1,0:T(8,128)(2,1)}, f32[1,32]{1,0:T(1,128)}, bf16[4,128,512]{2,1,0:T(8,128)(2,1)}) custom-call(bf16[16,3584]{1,0:T(8,128)(2,1)} %x_ref.1, s32[8,16]{1,0:T(8,128)} %bitcast.3, f32[8,16]{1,0:T(8,128)} %bitcast.4, s32[4]{0:T(128)} %lengths_ref.1, bf16[1,3584,2048]{2,1,0:T(8,128)(2,1)} %gate_up_hbm.1, ...), custom_call_target="tpu_custom_call" | custom-call | tf_op jit(solution)/shard_map/experts_and_attention/pallas_call | solution.py:338
  79.1 1.6 %copy.16 = bf16[16,3584]{1,0:T(8,128)(2,1)} copy(bf16[16,3584]{1,0:T(8,128)(2,1)} %get-tuple-element.12) | data formatting | bytes 229376
  80.6 1.1 %copy.17 = f32[32]{0:T(128)} copy(f32[32]{0:T(128)} %bitcast.5) | data formatting | bytes 256
  81.8 1.9 %copy.18 = bf16[4,128,512]{2,1,0:T(8,128)(2,1)} copy(bf16[4,128,512]{2,1,0:T(8,128)(2,1)} %get-tuple-element.14) | data formatting | bytes 1048576

commit v4 on v3

--- a/solution.py
+++ b/solution.py
@@ -7,7 +7,7 @@
 from jax.experimental.pallas import tpu as pltpu
 from jax.sharding import PartitionSpec as P
 
-WIDTH = 256
+WIDTH = 512
 MESH = pl.DeviceIdType.MESH
 F32 = jnp.float32
 BF16 = jnp.bfloat16
@@ -127,7 +127,9 @@
 
     pieces = [table_buf] + [rows_buf.at[c] for c in range(chunks)]
     line_copies, own, fwd, sibs = {}, {}, {}, {}
-    for i, buf in enumerate(pieces):
+
+    def stage_start(i):
+        buf = pieces[i]
         line_copies[i] = [
             send(buf.at[k, s, m], buf.at[k, s, m], line_send.at[i, j - 1], line_recv.at[i, j - 1], on_line(j))
             for j in range(1, line)
@@ -141,18 +143,16 @@
         for copy in line_copies[i]:
             copy.wait_recv()
         own[i] = [hop(i, s, 0, across[1]), hop(i, s, 1, across[2])]
-        sibs[i] = [hop(i, s, 3, sib)]
 
     def stage_cross(i):
         own[i][i % 2].wait_recv()
         fwd[i] = hop(i, secs[1 + i % 2], 2, across[2 - i % 2])
-        sibs[i].append(hop(i, secs[1 + i % 2], 4, sib))
         own[i][1 - i % 2].wait_recv()
-        sibs[i].append(hop(i, secs[2 - i % 2], 5, sib))
 
     def stage_diagonal(i):
         fwd[i].wait_recv()
-        sibs[i].append(hop(i, secs[3], 6, sib))
+        buf = pieces[i]
+        sibs[i] = send(buf.at[k], buf.at[k], hop_send.at[i, 3], hop_recv.at[i, 3], sib)
 
     def routing():
         part = 8 * rows
@@ -188,8 +188,7 @@
         att_ref[r] = jnp.dot(weights, lat[r], preferred_element_type=F32).astype(BF16)
 
     def stage_up(i):
-        for copy in sibs[i]:
-            copy.wait_recv()
+        sibs[i].wait_recv()
         if i == 0:
             routing()
             return
@@ -209,17 +208,21 @@
                 projected[:, cols] += part
 
     count = chunks + 1
+    for i in range(3):
+        stage_start(i)
     for copy in att_copies:
         copy.wait()
     att_rows = ql.shape[0]
     attended = 0
-    for i in range(count + 5):
+    for i in range(count + 4):
         if i < count:
+            if i + 3 < count:
+                stage_start(i + 3)
             stage_own(i)
-        if 0 <= i - 2 < count:
-            stage_cross(i - 2)
-        if 0 <= i - 4 < count:
-            stage_diagonal(i - 4)
+        if 0 <= i - 1 < count:
+            stage_cross(i - 1)
+        if 0 <= i - 3 < count:
+            stage_diagonal(i - 3)
         if len(gate_copies) < chunks:
             fetch_gate()
         if i == 4:
@@ -227,8 +230,8 @@
         if attended < att_rows and i >= 1:
             attend(attended)
             attended += 1
-        if 0 <= i - 5 < count:
-            stage_up(i - 5)
+        if 0 <= i - 4 < count:
+            stage_up(i - 4)
     for r in range(attended, att_rows):
         attend(r)
     for copy in started:
@@ -365,8 +368,8 @@
             dma((chunks + 5,)),
             dma((pieces, line - 1)),
             dma((pieces, line - 1)),
-            dma((pieces, 7)),
-            dma((pieces, 7)),
+            dma((pieces, 4)),
+            dma((pieces, 4)),
             dma((chunks, 4)),
             dma((chunks, 4)),
             dma((chunks, line - 1)),

time: 83.8 us -> 70.8 us (0.84)
  Pallas kernels: 78.4 us -> 65.3 us
    pallas_call x1, Pallas kernels: 78.4 us -> 65.3 us  [per_device(): pl.pallas_call(functools.partial(kernel, (capacity, top_count)), out_shap...]
where the time goes in v4:
time: 70.8 us; the launch traced here: 70.5 us
  Pallas kernels  65.3 us (92%)
  local copies, waits for them, and re-layouts  4.54 us (6%)
    pallas_call x1, Pallas kernels, per_device(): pl.pallas_call(functools.partial(kernel, (capacity, top_count)), out_shap...  65.3 us
    unnamed x3, local copies, waits for them, and re-layouts  4.54 us

profile of v4, /device:TPU:0, one launch (start us, length us, event | category | flops | bytes accessed | tf_op | source)
XLA Modules:
  0.0 70.5 jit_solution(7365421663117446008)
XLA Ops:
  0.6 65.3 %experts_and_attention.1 = (bf16[16,3584]{1,0:T(8,128)(2,1)}, f32[1,32]{1,0:T(1,128)}, bf16[4,128,512]{2,1,0:T(8,128)(2,1)}) custom-call(bf16[16,3584]{1,0:T(8,128)(2,1)} %x_ref.1, s32[8,16]{1,0:T(8,128)} %bitcast.3, f32[8,16]{1,0:T(8,128)} %bitcast.4, s32[4]{0:T(128)} %lengths_ref.1, bf16[1,3584,2048]{2,1,0:T(8,128)(2,1)} %gate_up_hbm.1, ...), custom_call_target="tpu_custom_call" | custom-call | tf_op jit(solution)/shard_map/experts_and_attention/pallas_call | solution.py:341
  66.0 1.6 %copy.16 = bf16[16,3584]{1,0:T(8,128)(2,1)} copy(bf16[16,3584]{1,0:T(8,128)(2,1)} %get-tuple-element.12) | data formatting | bytes 229376
  67.5 1.1 %copy.17 = f32[32]{0:T(128)} copy(f32[32]{0:T(128)} %bitcast.5) | data formatting | bytes 256
  68.7 1.9 %copy.18 = bf16[4,128,512]{2,1,0:T(8,128)(2,1)} copy(bf16[4,128,512]{2,1,0:T(8,128)(2,1)} %get-tuple-element.14) | data formatting | bytes 1048576
